TPU v7x, 512 devices: a whole 4x8x8 slice. The times are simulated.
512 devices in a mesh: leaf: 8 (over x, core), sub: 64 (over z, y).
Axes of the slice: x: 4, y: 8, z: 8, core: 2. Of those that a mesh axis runs over, the one named last changes fastest.
Arguments:
- points: bfloat16 [131072, 64], P(('leaf', 'sub')), may hold values from -6 to 6
- omega: bfloat16 [131072, 256], P(('leaf', 'sub')), may hold values from -6 to 6
- samples: float32 [131072, 256], P(('leaf', 'sub')), may hold values from -48 to 48
- ranks: int32 [8, 4], P('leaf'), may hold values from 128 to 256, as said below
- leaf_skeleton: int32 [8, 256], P('leaf'), may hold values from 0 to 16383, as said below
- merge_skeleton: int32 [8, 3, 256], P('leaf'), may hold values from 0 to 511, as said below
Outputs:
- leaf_interp: float32 [131072, 256], P(('leaf', 'sub'))
- node_interp: float32 [8, 3, 512, 256], P('leaf')
- couplings: float32 [8, 3, 256, 256], P('leaf')
- top_compressed: float32 [8, 256, 256], P('leaf')
Inputs may be any that keep to these rules, and one draw needn't show every extreme that they name: ranks[i, l] is the rank of the level-l node holding leaf i (leaves with equal i >> l share it); 256 is reached. `leaf_skeleton`: row i lists 256 distinct point indices within leaf i; the first ranks[i, 0] are its skeleton. merge_skeleton[i, l - 1] lists 256 distinct candidate rows of the level-l node holding leaf i, equal for all its leaves; candidate j < 256 is the lower child's row j, else the upper child's row j - 256; the first ranks[i, l] name rows below the owning child's rank.
All inputs are finite; a program needn't handle non-finite values.
Results may differ from a plain program's by a relative error of at most 0.00076.
Values may be sent and summed in bfloat16 or wider, within the bound.
A program may use at most 128 MiB of HBM per device.

v0:
```python
import jax
import jax.numpy as jnp
from jax import lax
from jax.sharding import PartitionSpec as P

LEVELS = 3


def partner(value, axis, stride):
    mask = 2**stride
    pairs = [(source, source ^ mask) for source in range(lax.axis_size(axis))]
    return lax.ppermute(value, axis, pairs)


def kernel(left, right):
    cross = jnp.einsum("id,jd->ij", left, right, preferred_element_type=jnp.float32)
    left_sq = jnp.sum(jnp.square(left.astype(jnp.float32)), axis=1)
    right_sq = jnp.sum(jnp.square(right.astype(jnp.float32)), axis=1)
    return jnp.exp(-(left_sq[:, None] + right_sq[None, :] - 2.0 * cross) / (0.5 * left.shape[1]))


def factorize(picked):
    gram = jnp.dot(
        picked, picked.T, precision=lax.Precision.HIGHEST, preferred_element_type=jnp.float32
    )
    shift = jnp.sum(picked * picked) / picked.shape[0] + 1e-06
    return jnp.linalg.cholesky(gram + shift * jnp.eye(picked.shape[0], dtype=jnp.float32))


def interpolate(factor, candid, picked):
    right_side = jnp.einsum("rs,ns->rn", picked, candid, precision=lax.Precision.HIGHEST)
    return jax.scipy.linalg.cho_solve((factor, True), right_side).T


def shards(points, omega, samples, ranks, leaf_skeleton, merge_skeleton):
    rows = points.shape[0]
    width = leaf_skeleton.shape[1]
    sub_pos = lax.axis_index("sub")
    leaf_pos = lax.axis_index("leaf")
    weights = kernel(points, lax.all_gather(points, "sub", axis=0, tiled=True)).astype(jnp.bfloat16)
    diag = jnp.dot(
        weights,
        lax.all_gather(omega, "sub", axis=0, tiled=True),
        preferred_element_type=jnp.float32,
    )
    resid = samples - diag
    live = (jnp.arange(width) < ranks[0, 0]).astype(jnp.float32)
    offsets = leaf_skeleton[0] - sub_pos * rows
    owned = ((offsets >= 0) & (offsets < rows)).astype(jnp.float32) * live
    places = jnp.clip(offsets, 0, rows - 1)
    part_rows = jnp.take(resid, places, axis=0) * owned[:, None]
    part_points = jnp.take(points, places, axis=0).astype(jnp.float32) * owned[:, None]
    omega_wide = omega.astype(jnp.float32)
    picked, chosen = lax.psum((part_rows, part_points), "sub")
    factor = factorize(picked)
    leaf_interp = interpolate(factor, resid, picked)
    local_part = jnp.einsum("nr,ns->rs", leaf_interp, omega_wide, precision=lax.Precision.HIGHEST)
    compressed = lax.psum(local_part, "sub")
    interp_levels = []
    couple_levels = []
    for height in range(1, LEVELS + 1):
        other_points, other_rows, other_comp, other_live = partner(
            (chosen, picked, compressed, live), "leaf", height - 1
        )
        coupling = (
            live[:, None]
            * other_live[None, :]
            * kernel(chosen.astype(jnp.bfloat16), other_points.astype(jnp.bfloat16))
        )
        own_new = picked - jnp.dot(coupling, other_comp, precision=lax.Precision.HIGHEST)
        other_new = other_rows - jnp.einsum(
            "ij,is->js", coupling, compressed, precision=lax.Precision.HIGHEST
        )
        is_lower = leaf_pos // 2 ** (height - 1) % 2 == 0
        cand_y = jnp.where(
            is_lower,
            jnp.concatenate([own_new, other_new], axis=0),
            jnp.concatenate([other_new, own_new], axis=0),
        )
        cand_x = jnp.where(
            is_lower,
            jnp.concatenate([chosen, other_points], axis=0),
            jnp.concatenate([other_points, chosen], axis=0),
        )
        cand_o = jnp.where(
            is_lower,
            jnp.concatenate([compressed, other_comp], axis=0),
            jnp.concatenate([other_comp, compressed], axis=0),
        )
        live = (jnp.arange(width) < ranks[0, height]).astype(jnp.float32)
        indices = merge_skeleton[0, height - 1]
        picked = jnp.take(cand_y, indices, axis=0) * live[:, None]
        chosen = jnp.take(cand_x, indices, axis=0) * live[:, None]
        factor = factorize(picked)
        node_matrix = interpolate(factor, cand_y, picked)
        compressed = jnp.einsum("nr,ns->rs", node_matrix, cand_o, precision=lax.Precision.HIGHEST)
        interp_levels.append(node_matrix)
        couple_levels.append(coupling)
    node_interp = jnp.stack(interp_levels, axis=0)[None]
    couplings = jnp.stack(couple_levels, axis=0)[None]
    return (leaf_interp, node_interp, couplings, compressed[None])


def solution(mesh):
    in_specs = (
        P(("leaf", "sub"), None),
        P(("leaf", "sub"), None),
        P(("leaf", "sub"), None),
        P("leaf", None),
        P("leaf", None),
        P("leaf", None, None),
    )
    out_specs = (
        P(("leaf", "sub"), None),
        P("leaf", None, None, None),
        P("leaf", None, None, None),
        P("leaf", None, None),
    )
    return jax.shard_map(shards, mesh=mesh, in_specs=in_specs, out_specs=out_specs, check_vma=False)
```

profile of v0, /device:TPU:16, one launch (start us, length us, event | category | flops | bytes accessed | tf_op | source)
XLA Modules:
  0.0 845.5 jit_solution(15058260484745908838)
XLA Ops:
  8.7 1.4 fusion.131
  10.8 1.9 collective-permute-start
  13.3 3.4 collective-permute-start.4
  17.4 4.6 collective-permute-start.8
  26.3 71.9 %all-gather.3.cloned.1.call-done = bf16[16384,64]{0,1:T(8,128)(2,1)} async-done(((bf16[256,64]{0,1:T(8,128)(2,1)}), bf16[16384,64]{0,1:T(8,128)(2,1)}) %all-gather.3.cloned.1.call-update) | async-done | bytes 2097168 | tf_op jit(solution)/shard_map/all_gather | solution.py:40
  98.2 2.1 multiply_reduce_fusion
  100.3 96.8 %all-gather.5.cloned.1.call-done = bf16[16384,256]{1,0:T(8,128)(2,1)} async-done(((bf16[256,256]{1,0:T(8,128)(2,1)}), bf16[16384,256]{1,0:T(8,128)(2,1)}) %all-gather.5.cloned.1.call-update) | async-done | bytes 8388624 | tf_op jit(solution)/shard_map/all_gather | solution.py:43
  197.1 8.7 %fusion.6 = f32[256,256]{1,0:T(8,128)S(1)} fusion(f32[256,256]{1,0:T(8,128)} %param.15, bf16[16384,256]{1,0:T(8,128)(2,1)} %all-gather.5.cloned.1.call-done, bf16[256,64]{0,1:T(8,128)(2,1)} %param.13, bf16[16384,64]{0,1:T(8,128)(2,1)} %all-gather.3.cloned.1.call-done, f32[16384]{0:T(1024)S(1)} %multiply_reduce_fusion, f32[256]{0:T(256)S(1)} %multiply_reduce_fusion.11), kind=kOutput, calls=%fused_computation.24 | convolution fusion | flops 2709585920 | bytes 11109376 | tf_op jit(solution)/shard_map/dot_general | solution.py:41
  209.8 148.1 %all-reduce.5.cloned.1.call-done = f32[256,256]{1,0:T(8,128)} async-done(((f32[256,256]{1,0:T(8,128)}), f32[256,256]{1,0:T(8,128)}) %all-reduce.5.cloned.1.call-update) | async-done | bytes 262160 | tf_op jit(solution)/shard_map/psum | solution.py:54
  357.9 1.7 multiply_reduce_fusion.4
  360.3 1.4 convolution_add_fusion.3
  361.9 11.7 %cholesky.214 = f32[128,128]{1,0:T(8,128)S(1)} custom-call(f32[128,128]{1,0:T(8,128)S(1)} %cholesky.346), custom_call_target="Cholesky" | custom-call | tf_op jit(solution)/shard_map/jit(cholesky)/cholesky | solution.py:27
  373.8 9.8 %custom-call.26 = f32[1,128,128]{1,2,0:T(8,128)S(1)} custom-call(f32[1,128,128]{2,1,0:T(8,128)S(1)} %get-tuple-element.120), custom_call_target="InvertDiagBlocksLowerTriangular" | custom-call | tf_op jit(solution)/shard_map/jit(cholesky)/cholesky | solution.py:27
  384.2 11.7 %cholesky.231 = f32[128,128]{1,0:T(8,128)S(1)} custom-call(f32[128,128]{1,0:T(8,128)S(1)} %convolution_subtract_fusion.17), custom_call_target="Cholesky" | custom-call | tf_op jit(solution)/shard_map/jit(cholesky)/cholesky | solution.py:27
  398.3 4.6 while.7
  399.1 1.4 dynamic-slice.26
  401.3 1.4 dynamic-slice.26
  402.8 19.7 %custom-call.20 = f32[2,128,128]{1,2,0:T(8,128)S(1)} custom-call(f32[2,128,128]{2,1,0:T(8,128)S(1)} %get-tuple-element.23), custom_call_target="InvertDiagBlocksLowerTriangular" | custom-call | tf_op jit(solution)/shard_map/jit(_cho_solve)/triangular_solve | solution.py:32
  422.5 1.4 fusion.132
  425.6 1.0 fusion.52
  427.5 1.9 collective-permute-start.3
  429.4 148.6 %all-reduce.7.cloned.1.call-done = (f32[256,256]{1,0:T(8,128)}, f32[256,64]{1,0:T(8,128)}) async-done(((f32[256,256]{1,0:T(8,128)}, f32[256,64]{1,0:T(8,128)}), (f32[256,256]{1,0:T(8,128)}, f32[256,64]{1,0:T(8,128)})) %all-reduce.7.cloned.1.call-update) | async-done | bytes 327696 | tf_op jit(solution)/shard_map/psum | solution.py:58
  578.0 1.9 collective-permute-start.1
  580.0 1.0 multiply_reduce_fusion.10
  581.5 2.0 collective-permute-start.2
  583.6 1.1 fusion.18
  584.8 1.0 maximum_select_fusion.9
  586.7 3.4 collective-permute-start.5
  590.1 1.6 convolution_subtract_fusion.10
  591.9 2.5 collective-permute-done.5
  595.4 4.9 collective-permute-start.9
  600.6 2.4 collective-permute-done.9
  605.6 3.8 collective-permute-start.7
  611.3 11.7 %cholesky.248 = f32[128,128]{1,0:T(8,128)S(1)} custom-call(f32[128,128]{1,0:T(8,128)S(1)} %cholesky.349), custom_call_target="Cholesky" | custom-call | tf_op jit(solution)/shard_map/jit(cholesky)/cholesky | solution.py:27
  623.0 9.8 %custom-call.27 = f32[1,128,128]{1,2,0:T(8,128)S(1)} custom-call(f32[1,128,128]{2,1,0:T(8,128)S(1)} %get-tuple-element.118), custom_call_target="InvertDiagBlocksLowerTriangular" | custom-call | tf_op jit(solution)/shard_map/jit(cholesky)/cholesky | solution.py:27
  633.3 11.7 %cholesky.265 = f32[128,128]{1,0:T(8,128)S(1)} custom-call(f32[128,128]{1,0:T(8,128)S(1)} %convolution_subtract_fusion.16), custom_call_target="Cholesky" | custom-call | tf_op jit(solution)/shard_map/jit(cholesky)/cholesky | solution.py:27
  647.7 4.2 while.8
  648.5 1.4 bitcast_dynamic-update-slice_fusion.9
  650.5 1.4 bitcast_dynamic-update-slice_fusion.9
  651.9 19.7 %custom-call.28 = f32[2,128,128]{1,2,0:T(8,128)S(1)} custom-call(f32[2,128,128]{2,1,0:T(8,128)S(1)} %get-tuple-element.36), custom_call_target="InvertDiagBlocksLowerTriangular" | custom-call | tf_op jit(solution)/shard_map/jit(_cho_solve)/triangular_solve | solution.py:32
  674.6 2.5 collective-permute-start.6
  677.8 5.1 collective-permute-done.6
  685.2 4.8 collective-permute-start.11
  691.9 11.7 %cholesky.282 = f32[128,128]{1,0:T(8,128)S(1)} custom-call(f32[128,128]{1,0:T(8,128)S(1)} %cholesky.352), custom_call_target="Cholesky" | custom-call | tf_op jit(solution)/shard_map/jit(cholesky)/cholesky | solution.py:27
  703.6 9.8 %custom-call.29 = f32[1,128,128]{1,2,0:T(8,128)S(1)} custom-call(f32[1,128,128]{2,1,0:T(8,128)S(1)} %get-tuple-element.114), custom_call_target="InvertDiagBlocksLowerTriangular" | custom-call | tf_op jit(solution)/shard_map/jit(cholesky)/cholesky | solution.py:27
  713.9 11.7 %cholesky.299 = f32[128,128]{1,0:T(8,128)S(1)} custom-call(f32[128,128]{1,0:T(8,128)S(1)} %convolution_subtract_fusion.15), custom_call_target="Cholesky" | custom-call | tf_op jit(solution)/shard_map/jit(cholesky)/cholesky | solution.py:27
  728.4 4.5 while.9
  729.4 1.3 bitcast_dynamic-update-slice_fusion.10
  731.5 1.3 bitcast_dynamic-update-slice_fusion.10
  732.8 19.7 %custom-call.30 = f32[2,128,128]{1,2,0:T(8,128)S(1)} custom-call(f32[2,128,128]{2,1,0:T(8,128)S(1)} %get-tuple-element.37), custom_call_target="InvertDiagBlocksLowerTriangular" | custom-call | tf_op jit(solution)/shard_map/jit(_cho_solve)/triangular_solve | solution.py:32
  754.9 1.8 fusion.25
  756.7 2.8 collective-permute-start.10
  760.5 1.6 convolution_subtract_fusion.2
  762.1 4.5 collective-permute-done.10
  766.6 1.4 convolution_subtract_fusion.3
  771.7 11.7 %cholesky.316 = f32[128,128]{1,0:T(8,128)S(1)} custom-call(f32[128,128]{1,0:T(8,128)S(1)} %cholesky.355), custom_call_target="Cholesky" | custom-call | tf_op jit(solution)/shard_map/jit(cholesky)/cholesky | solution.py:27
  783.5 9.8 %custom-call.31 = f32[1,128,128]{1,2,0:T(8,128)S(1)} custom-call(f32[1,128,128]{2,1,0:T(8,128)S(1)} %get-tuple-element.110), custom_call_target="InvertDiagBlocksLowerTriangular" | custom-call | tf_op jit(solution)/shard_map/jit(cholesky)/cholesky | solution.py:27
  793.8 11.9 %cholesky.333 = f32[128,128]{1,0:T(8,128)S(1)} custom-call(f32[128,128]{1,0:T(8,128)S(1)} %convolution_subtract_fusion.14), custom_call_target="Cholesky" | custom-call | tf_op jit(solution)/shard_map/jit(cholesky)/cholesky | solution.py:27
  808.5 4.1 while.10
  809.1 1.4 bitcast_dynamic-update-slice_fusion.11
  811.1 1.4 bitcast_dynamic-update-slice_fusion.11
  812.6 19.7 %custom-call.32 = f32[2,128,128]{1,2,0:T(8,128)S(1)} custom-call(f32[2,128,128]{2,1,0:T(8,128)S(1)} %get-tuple-element.38), custom_call_target="InvertDiagBlocksLowerTriangular" | custom-call | tf_op jit(solution)/shard_map/jit(_cho_solve)/triangular_solve | solution.py:32
  834.8 1.6 copy.39
  836.5 2.3 convolution_bitcast_fusion
  (187 shorter events, 49.6 us)
Async XLA Ops:
  7.2 91.0 %all-gather.3.cloned.1.call-start = ((), (), s32[]{:S(2)}) async-start(), calls=%async_computation | async-start | bytes 2129920 | tf_op jit(solution)/shard_map/all_gather | solution.py:40
  7.9 189.2 %all-gather.5.cloned.1.call-start = ((), (), s32[]{:S(2)}) async-start(), calls=%async_computation.1 | async-start | bytes 8519680 | tf_op jit(solution)/shard_map/all_gather | solution.py:43
  8.6 349.3 %all-reduce.5.cloned.1.call-start = ((), (), s32[]{:S(2)}) async-start(), calls=%async_computation.2 | async-start | bytes 524288 | tf_op jit(solution)/shard_map/psum | solution.py:54
  10.8 576.0 %collective-permute-start = (f32[256]{0:T(256)S(1)}, f32[256]{0:T(256)S(1)}, u32[]{:S(2)}, u32[]{:S(2)}) collective-permute-start(f32[256]{0:T(256)S(1)} %fusion.116), channel_id=1, source_target_pairs={{0,64},{64,0},{128,192},{192,128},{256,320},{320,256},{384,448},{4... | collective-permute-start | bytes 3080 | tf_op jit(solution)/shard_map/ppermute | solution.py:12
  13.3 591.5 %collective-permute-start.4 = (f32[256]{0:T(256)S(1)}, f32[256]{0:T(256)S(1)}, u32[]{:S(2)}, u32[]{:S(2)}) collective-permute-start(f32[256]{0:T(256)S(1)} %compare_convert_fusion.2), channel_id=1, source_target_pairs={{0,128},{64,192},{128,0},{192,64},{256,384},{320,448},{384,256},{4... | collective-permute-start | bytes 3080 | tf_op jit(solution)/shard_map/ppermute | solution.py:12
  17.4 666.9 %collective-permute-start.8 = (f32[256]{0:T(256)S(1)}, f32[256]{0:T(256)S(1)}, u32[]{:S(2)}, u32[]{:S(2)}) collective-permute-start(f32[256]{0:T(256)S(1)} %compare_convert_fusion.1), channel_id=1, source_target_pairs={{0,256},{64,320},{128,384},{192,448},{256,0},{320,64},{384,128},{4... | collective-permute-start | bytes 3080 | tf_op jit(solution)/shard_map/ppermute | solution.py:12
  100.3 107.7 %copy-start.2 = (bf16[256,64]{0,1:T(8,128)(2,1)S(1)}, bf16[256,64]{0,1:T(8,128)(2,1)}, u32[]{:S(2)}) copy-start(bf16[256,64]{0,1:T(8,128)(2,1)} %param.13) | copy-start | bytes 98308
  205.9 219.8 %copy-start.1 = (bf16[256,256]{1,0:T(8,128)(2,1)S(1)}, bf16[256,256]{1,0:T(8,128)(2,1)}, u32[]{:S(2)}) copy-start(bf16[256,256]{1,0:T(8,128)(2,1)} %param.14) | copy-start | bytes 393220
  207.7 370.3 %all-reduce.7.cloned.1.call-start = ((), (), s32[]{:S(2)}) async-start(), calls=%async_computation.3 | async-start | bytes 786432 | tf_op jit(solution)/shard_map/psum | solution.py:58
  357.9 69.6 %copy-start = (f32[256,256]{1,0:T(8,128)S(1)}, f32[256,256]{1,0:T(8,128)}, u32[]{:S(2)}) copy-start(f32[256,256]{1,0:T(8,128)} %all-reduce.5.cloned.1.call-done) | copy-start | bytes 786436
  427.5 162.6 %collective-permute-start.3 = (f32[256,256]{1,0:T(8,128)S(1)}, f32[256,256]{1,0:T(8,128)S(1)}, u32[]{:S(2)}, u32[]{:S(2)}) collective-permute-start(f32[256,256]{1,0:T(8,128)S(1)} %copy-done), channel_id=1, source_target_pairs={{0,64},{64,0},{128,192},{192,128},{256,320},{320,256},{384,448},{4... | collective-permute-start | bytes 786440 | tf_op jit(solution)/shard_map/ppermute | solution.py:12
  578.0 3.4 collective-permute-start.1
  581.5 21.9 %collective-permute-start.2 = (f32[256,256]{1,0:T(8,128)}, f32[256,256]{1,0:T(8,128)S(1)}, u32[]{:S(2)}, u32[]{:S(2)}) collective-permute-start(f32[256,256]{1,0:T(8,128)} %get-tuple-element.87), channel_id=1, source_target_pairs={{0,64},{64,0},{128,192},{192,128},{256,320},{320,256},{384,448},{4... | collective-permute-start | bytes 786440 | tf_op jit(solution)/shard_map/ppermute | solution.py:12
  586.7 7.7 collective-permute-start.5
  595.4 7.7 collective-permute-start.9
  600.4 73.6 %copy-start.3 = (f32[256,256]{1,0:T(8,128)S(1)}, f32[256,256]{1,0:T(8,128)}, u32[]{:S(2)}) copy-start(f32[256,256]{1,0:T(8,128)} %get-tuple-element.87) | copy-start | bytes 786436
  605.6 71.6 %collective-permute-start.7 = (f32[256,256]{1,0:T(8,128)S(1)}, f32[256,256]{1,0:T(8,128)S(1)}, u32[]{:S(2)}, u32[]{:S(2)}) collective-permute-start(f32[256,256]{1,0:T(8,128)S(1)} %get-tuple-element.96), channel_id=1, source_target_pairs={{0,128},{64,192},{128,0},{192,64},{256,384},{320,448},{384,256},{4... | collective-permute-start | bytes 786440 | tf_op jit(solution)/shard_map/ppermute | solution.py:12
  674.6 3.2 copy-start.4
  674.6 8.3 collective-permute-start.6
  682.9 2.3 copy-start.5
  685.2 75.3 %collective-permute-start.11 = (f32[256,256]{1,0:T(8,128)S(1)}, f32[256,256]{1,0:T(8,128)}, u32[]{:S(2)}, u32[]{:S(2)}) collective-permute-start(f32[256,256]{1,0:T(8,128)S(1)} %get-tuple-element.92), channel_id=1, source_target_pairs={{0,256},{64,320},{128,384},{192,448},{256,0},{320,64},{384,128},{4... | collective-permute-start | bytes 786440 | tf_op jit(solution)/shard_map/ppermute | solution.py:12
  756.7 9.9 %collective-permute-start.10 = (f32[256,256]{1,0:T(8,128)S(1)}, f32[256,256]{1,0:T(8,128)}, u32[]{:S(2)}, u32[]{:S(2)}) collective-permute-start(f32[256,256]{1,0:T(8,128)S(1)} %fusion.25), channel_id=1, source_target_pairs={{0,256},{64,320},{128,384},{192,448},{256,0},{320,64},{384,128},{4... | collective-permute-start | bytes 786440 | tf_op jit(solution)/shard_map/ppermute | solution.py:12
Sparse Core Ops, SparseCore 0:
  11.0 87.1 all-gather.2
  101.3 95.8 all-gather.4
  207.8 150.0 all-reduce.4
  426.8 151.2 all-reduce.6
where the time goes:
time: 852 us; the launch traced here: 846 us
  waiting for transfers between devices  482 us (57%)
  other arithmetic  235 us (28%)
  matrix products  38.8 us (5%)
  starting transfers between devices  38.2 us (4%)
  local copies, waits for them, and re-layouts  28.2 us (3%)
  between operations  23 us (3%)
    psum x1, waiting for transfers between devices, shards(): compressed = lax.psum(local_part, 'sub')  149 us
    psum x1, waiting for transfers between devices, shards(): picked, chosen = lax.psum((part_rows, part_points), 'sub')  148 us
    another operation x27, other arithmetic, factorize(): jnp.linalg.cholesky(gram + shift * jnp.eye(picked.shape[0], dtype=jnp.flo...  138 us
    all_gather x1, waiting for transfers between devices, shards(): lax.all_gather(omega, 'sub', axis=0, tiled=True)  96.8 us
    another operation x9, other arithmetic, interpolate(): return jax.scipy.linalg.cho_solve((factor, True), right_side).T  78.8 us
    all_gather x1, waiting for transfers between devices, shards(): lax.all_gather(points, 'sub', axis=0, tiled=True)  71.9 us
    ppermute x12, starting transfers between devices, partner(): return lax.ppermute(value, axis, pairs)  37.9 us
  transfers between devices with their start and end apart: 16, of which 9 were waited for; matrix products, arithmetic and copies ran while one was open for 27% of the time, Pallas kernels for 0%

commit v1 on v0

--- a/solution.py
+++ b/solution.py
@@ -37,7 +37,12 @@
     width = leaf_skeleton.shape[1]
     sub_pos = lax.axis_index("sub")
     leaf_pos = lax.axis_index("leaf")
-    weights = kernel(points, lax.all_gather(points, "sub", axis=0, tiled=True)).astype(jnp.bfloat16)
+    weights = kernel(
+        points,
+        jnp.concatenate(
+            lax.all_to_all(jnp.stack([points] * lax.axis_size("sub")), "sub", 0, 0), axis=0
+        ),
+    ).astype(jnp.bfloat16)
     diag = jnp.dot(
         weights,
         lax.all_gather(omega, "sub", axis=0, tiled=True),

time: 852 us -> 809 us (0.950)
  waiting for transfers between devices: 482 us -> 420 us
  starting transfers between devices: 38.2 us -> 54 us
    all_gather x1 -> x0, waiting for transfers between devices: 71.9 us -> none  [shards(): lax.all_gather(points, 'sub', axis=0, tiled=True)]
    all_to_all x0 -> x1, waiting for transfers between devices: none -> 34.5 us  [shards(): lax.all_to_all(jnp.stack([points] * lax.axis_size('sub')), 'sub', 0, 0)]
    all_gather x1, waiting for transfers between devices: 96.8 us -> 69.9 us  [shards(): lax.all_gather(omega, 'sub', axis=0, tiled=True)]
    all_to_all x0 -> x1, starting transfers between devices: none -> 16.5 us  [shards(): lax.all_to_all(jnp.stack([points] * lax.axis_size('sub')), 'sub', 0, 0)]
  transfers between devices with their start and end apart: 16 -> 16, of which waited for: 9 -> 10; matrix products, arithmetic and copies ran while one was open for 27% -> 21% of each run, Pallas kernels for 0% -> 0%
where the time goes in v1:
time: 809 us; the launch traced here: 802 us
  waiting for transfers between devices  420 us (52%)
  other arithmetic  234 us (29%)
  starting transfers between devices  54 us (7%)
  matrix products  36.7 us (5%)
  local copies, waits for them, and re-layouts  33.3 us (4%)
  between operations  23 us (3%)
    psum x1, waiting for transfers between devices, shards(): compressed = lax.psum(local_part, 'sub')  149 us
    psum x1, waiting for transfers between devices, shards(): picked, chosen = lax.psum((part_rows, part_points), 'sub')  148 us
    another operation x27, other arithmetic, factorize(): jnp.linalg.cholesky(gram + shift * jnp.eye(picked.shape[0], dtype=jnp.flo...  139 us
    another operation x9, other arithmetic, interpolate(): return jax.scipy.linalg.cho_solve((factor, True), right_side).T  78.8 us
    all_gather x1, waiting for transfers between devices, shards(): lax.all_gather(omega, 'sub', axis=0, tiled=True)  69.9 us
    ppermute x12, starting transfers between devices, partner(): return lax.ppermute(value, axis, pairs)  37.3 us
    all_to_all x1, waiting for transfers between devices, shards(): lax.all_to_all(jnp.stack([points] * lax.axis_size('sub')), 'sub', 0, 0)  34.5 us
    ppermute x12, waiting for transfers between devices, partner(): return lax.ppermute(value, axis, pairs)  18.2 us
  transfers between devices with their start and end apart: 16, of which 10 were waited for; matrix products, arithmetic and copies ran while one was open for 21% of the time, Pallas kernels for 0%

profile of v1, /device:TPU:16, one launch (start us, length us, event | category | flops | bytes accessed | tf_op | source)
XLA Modules:
  0.0 801.7 jit_solution(10409537255946701444)
XLA Ops:
  7.9 2.4 stack.18
  10.3 16.5 %all-to-all-start = ((bf16[64,256,64]{1,2,0:T(8,128)(2,1)}), bf16[64,256,64]{1,2,0:T(8,128)(2,1)S(1)}, u32[]{:S(2)}, u32[]{:S(2)}) async-start(bf16[64,256,64]{1,2,0:T(8,128)(2,1)} %stack.18), calls=%async_computation | async-start | bytes 4194304 | tf_op jit(solution)/shard_map/all_to_all | solution.py:43
  26.9 1.4 fusion.131
  28.9 1.9 collective-permute-start
  31.5 3.4 collective-permute-start.4
  35.6 4.6 collective-permute-start.8
  43.8 1.2 compare_and_fusion
  45.1 34.5 %all-to-all-done = bf16[64,256,64]{1,2,0:T(8,128)(2,1)S(1)} async-done(((bf16[64,256,64]{1,2,0:T(8,128)(2,1)}), bf16[64,256,64]{1,2,0:T(8,128)(2,1)S(1)}, u32[]{:S(2)}, u32[]{:S(2)}) %all-to-all-start) | async-done | bytes 2097184 | tf_op jit(solution)/shard_map/all_to_all | solution.py:43
  79.5 1.5 copy.78
  81.8 69.9 %all-gather.2.cloned.1.call-done = bf16[16384,256]{1,0:T(8,128)(2,1)} async-done(((bf16[256,256]{1,0:T(8,128)(2,1)}), bf16[16384,256]{1,0:T(8,128)(2,1)}) %all-gather.2.cloned.1.call-update) | async-done | bytes 8388624 | tf_op jit(solution)/shard_map/all_gather | solution.py:48
  151.7 8.7 %fusion.6 = f32[256,256]{1,0:T(8,128)S(1)} fusion(f32[256,256]{1,0:T(8,128)S(1)} %copy-done.9, bf16[16384,256]{1,0:T(8,128)(2,1)} %all-gather.2.cloned.1.call-done, bf16[256,64]{0,1:T(8,128)(2,1)S(1)} %copy-done.2, bf16[16384,64]{0,1:T(8,128)(2,1)} %bitcast.210, f32[16384]{0:T(1024)S(1)} %bitcast.212, f32[256]{0:T(256)S(1)} %multiply_reduce_fusion.11), kind=kOutput, calls=%fused_computation.24 | convolution fusion | flops 2709585920 | bytes 11109376 | tf_op jit(solution)/shard_map/dot_general | solution.py:46
  164.4 148.0 %all-reduce.5.cloned.1.call-done = f32[256,256]{1,0:T(8,128)} async-done(((f32[256,256]{1,0:T(8,128)}), f32[256,256]{1,0:T(8,128)}) %all-reduce.5.cloned.1.call-update) | async-done | bytes 262160 | tf_op jit(solution)/shard_map/psum | solution.py:59
  312.3 1.7 multiply_reduce_fusion.4
  314.7 1.4 convolution_add_fusion.3
  316.3 11.7 %cholesky.214 = f32[128,128]{1,0:T(8,128)S(1)} custom-call(f32[128,128]{1,0:T(8,128)S(1)} %cholesky.346), custom_call_target="Cholesky" | custom-call | tf_op jit(solution)/shard_map/jit(cholesky)/cholesky | solution.py:27
  328.1 9.8 %custom-call.26 = f32[1,128,128]{1,2,0:T(8,128)S(1)} custom-call(f32[1,128,128]{2,1,0:T(8,128)S(1)} %get-tuple-element.136), custom_call_target="InvertDiagBlocksLowerTriangular" | custom-call | tf_op jit(solution)/shard_map/jit(cholesky)/cholesky | solution.py:27
  338.4 11.7 %cholesky.231 = f32[128,128]{1,0:T(8,128)S(1)} custom-call(f32[128,128]{1,0:T(8,128)S(1)} %convolution_subtract_fusion.17), custom_call_target="Cholesky" | custom-call | tf_op jit(solution)/shard_map/jit(cholesky)/cholesky | solution.py:27
  352.6 4.6 while.7
  353.6 1.4 dynamic-slice.26
  355.7 1.4 dynamic-slice.26
  357.2 19.7 %custom-call.20 = f32[2,128,128]{1,2,0:T(8,128)S(1)} custom-call(f32[2,128,128]{2,1,0:T(8,128)S(1)} %get-tuple-element.23), custom_call_target="InvertDiagBlocksLowerTriangular" | custom-call | tf_op jit(solution)/shard_map/jit(_cho_solve)/triangular_solve | solution.py:32
  376.9 1.4 fusion.132
  381.9 1.9 collective-permute-start.3
  383.8 148.6 %all-reduce.7.cloned.1.call-done = (f32[256,256]{1,0:T(8,128)}, f32[256,64]{1,0:T(8,128)}) async-done(((f32[256,256]{1,0:T(8,128)}, f32[256,64]{1,0:T(8,128)}), (f32[256,256]{1,0:T(8,128)}, f32[256,64]{1,0:T(8,128)})) %all-reduce.7.cloned.1.call-update) | async-done | bytes 327696 | tf_op jit(solution)/shard_map/psum | solution.py:63
  532.5 1.9 collective-permute-start.1
  535.9 2.0 collective-permute-start.2
  538.1 1.1 fusion.18
  539.2 1.0 maximum_select_fusion.9
  541.2 3.4 collective-permute-start.5
  544.6 1.6 convolution_subtract_fusion.10
  546.3 2.5 collective-permute-done.5
  549.8 4.9 collective-permute-start.9
  559.2 11.7 %cholesky.248 = f32[128,128]{1,0:T(8,128)S(1)} custom-call(f32[128,128]{1,0:T(8,128)S(1)} %cholesky.349), custom_call_target="Cholesky" | custom-call | tf_op jit(solution)/shard_map/jit(cholesky)/cholesky | solution.py:27
  570.9 9.8 %custom-call.27 = f32[1,128,128]{1,2,0:T(8,128)S(1)} custom-call(f32[1,128,128]{2,1,0:T(8,128)S(1)} %get-tuple-element.134), custom_call_target="InvertDiagBlocksLowerTriangular" | custom-call | tf_op jit(solution)/shard_map/jit(cholesky)/cholesky | solution.py:27
  581.2 11.9 %cholesky.265 = f32[128,128]{1,0:T(8,128)S(1)} custom-call(f32[128,128]{1,0:T(8,128)S(1)} %convolution_subtract_fusion.16), custom_call_target="Cholesky" | custom-call | tf_op jit(solution)/shard_map/jit(cholesky)/cholesky | solution.py:27
  595.8 4.0 while.8
  596.4 1.4 bitcast_dynamic-update-slice_fusion.9
  598.4 1.4 bitcast_dynamic-update-slice_fusion.9
  599.8 19.7 %custom-call.28 = f32[2,128,128]{1,2,0:T(8,128)S(1)} custom-call(f32[2,128,128]{2,1,0:T(8,128)S(1)} %get-tuple-element.36), custom_call_target="InvertDiagBlocksLowerTriangular" | custom-call | tf_op jit(solution)/shard_map/jit(_cho_solve)/triangular_solve | solution.py:32
  622.5 2.5 collective-permute-start.6
  625.1 3.4 collective-permute-start.7
  628.7 4.9 collective-permute-done.6
  634.1 3.4 collective-permute-done.7
  641.9 11.7 %cholesky.282 = f32[128,128]{1,0:T(8,128)S(1)} custom-call(f32[128,128]{1,0:T(8,128)S(1)} %cholesky.352), custom_call_target="Cholesky" | custom-call | tf_op jit(solution)/shard_map/jit(cholesky)/cholesky | solution.py:27
  653.7 9.8 %custom-call.29 = f32[1,128,128]{1,2,0:T(8,128)S(1)} custom-call(f32[1,128,128]{2,1,0:T(8,128)S(1)} %get-tuple-element.130), custom_call_target="InvertDiagBlocksLowerTriangular" | custom-call | tf_op jit(solution)/shard_map/jit(cholesky)/cholesky | solution.py:27
  664.0 12.1 %cholesky.299 = f32[128,128]{1,0:T(8,128)S(1)} custom-call(f32[128,128]{1,0:T(8,128)S(1)} %convolution_subtract_fusion.15), custom_call_target="Cholesky" | custom-call | tf_op jit(solution)/shard_map/jit(cholesky)/cholesky | solution.py:27
  678.8 5.5 while.9
  680.1 1.4 bitcast_dynamic-update-slice_fusion.10
  682.9 1.4 bitcast_dynamic-update-slice_fusion.10
  684.3 19.7 %custom-call.30 = f32[2,128,128]{1,2,0:T(8,128)S(1)} custom-call(f32[2,128,128]{2,1,0:T(8,128)S(1)} %get-tuple-element.37), custom_call_target="InvertDiagBlocksLowerTriangular" | custom-call | tf_op jit(solution)/shard_map/jit(_cho_solve)/triangular_solve | solution.py:32
  706.4 1.6 fusion.25
  708.1 2.8 collective-permute-start.10
  710.9 4.6 collective-permute-start.11
  716.5 4.3 collective-permute-done.10
  721.1 2.5 collective-permute-done.11
  728.1 11.7 %cholesky.316 = f32[128,128]{1,0:T(8,128)S(1)} custom-call(f32[128,128]{1,0:T(8,128)S(1)} %cholesky.355), custom_call_target="Cholesky" | custom-call | tf_op jit(solution)/shard_map/jit(cholesky)/cholesky | solution.py:27
  739.9 9.8 %custom-call.31 = f32[1,128,128]{1,2,0:T(8,128)S(1)} custom-call(f32[1,128,128]{2,1,0:T(8,128)S(1)} %get-tuple-element.126), custom_call_target="InvertDiagBlocksLowerTriangular" | custom-call | tf_op jit(solution)/shard_map/jit(cholesky)/cholesky | solution.py:27
  750.2 11.9 %cholesky.333 = f32[128,128]{1,0:T(8,128)S(1)} custom-call(f32[128,128]{1,0:T(8,128)S(1)} %convolution_subtract_fusion.14), custom_call_target="Cholesky" | custom-call | tf_op jit(solution)/shard_map/jit(cholesky)/cholesky | solution.py:27
  764.8 4.0 while.10
  765.4 1.4 bitcast_dynamic-update-slice_fusion.11
  767.4 1.4 bitcast_dynamic-update-slice_fusion.11
  768.8 19.7 %custom-call.32 = f32[2,128,128]{1,2,0:T(8,128)S(1)} custom-call(f32[2,128,128]{2,1,0:T(8,128)S(1)} %get-tuple-element.38), custom_call_target="InvertDiagBlocksLowerTriangular" | custom-call | tf_op jit(solution)/shard_map/jit(_cho_solve)/triangular_solve | solution.py:32
  791.0 1.6 copy.72
  792.7 2.3 convolution_bitcast_fusion
  (201 shorter events, 53.2 us)
Async XLA Ops:
  7.2 144.5 %copy-start.2 = (bf16[256,64]{0,1:T(8,128)(2,1)S(1)}, bf16[256,64]{0,1:T(8,128)(2,1)}, u32[]{:S(2)}) copy-start(bf16[256,64]{0,1:T(8,128)(2,1)} %param.13) | copy-start | bytes 98308
  7.2 144.5 %copy-start.9 = (f32[256,256]{1,0:T(8,128)S(1)}, f32[256,256]{1,0:T(8,128)}, u32[]{:S(2)}) copy-start(f32[256,256]{1,0:T(8,128)} %param.15) | copy-start | bytes 786436
  7.2 144.5 %all-gather.2.cloned.1.call-start = ((), (), s32[]{:S(2)}) async-start(), calls=%async_computation.1 | async-start | bytes 8519680 | tf_op jit(solution)/shard_map/all_gather | solution.py:48
  10.3 69.2 %all-to-all-start = ((bf16[64,256,64]{1,2,0:T(8,128)(2,1)}), bf16[64,256,64]{1,2,0:T(8,128)(2,1)S(1)}, u32[]{:S(2)}, u32[]{:S(2)}) async-start(bf16[64,256,64]{1,2,0:T(8,128)(2,1)} %stack.18), calls=%async_computation | async-start | bytes 4194304 | tf_op jit(solution)/shard_map/all_to_all | solution.py:43
  26.8 285.5 %all-reduce.5.cloned.1.call-start = ((), (), s32[]{:S(2)}) async-start(), calls=%async_computation.2 | async-start | bytes 524288 | tf_op jit(solution)/shard_map/psum | solution.py:59
  28.9 512.3 %collective-permute-start = (f32[256]{0:T(256)S(1)}, f32[256]{0:T(256)S(1)}, u32[]{:S(2)}, u32[]{:S(2)}) collective-permute-start(f32[256]{0:T(256)S(1)} %fusion.116), channel_id=1, source_target_pairs={{0,64},{64,0},{128,192},{192,128},{256,320},{320,256},{384,448},{4... | collective-permute-start | bytes 3080 | tf_op jit(solution)/shard_map/ppermute | solution.py:12
  31.5 525.0 %collective-permute-start.4 = (f32[256]{0:T(256)S(1)}, f32[256]{0:T(256)S(1)}, u32[]{:S(2)}, u32[]{:S(2)}) collective-permute-start(f32[256]{0:T(256)S(1)} %compare_convert_fusion.2), channel_id=1, source_target_pairs={{0,128},{64,192},{128,0},{192,64},{256,384},{320,448},{384,256},{4... | collective-permute-start | bytes 3080 | tf_op jit(solution)/shard_map/ppermute | solution.py:12
  35.6 603.7 %collective-permute-start.8 = (f32[256]{0:T(256)S(1)}, f32[256]{0:T(256)S(1)}, u32[]{:S(2)}, u32[]{:S(2)}) collective-permute-start(f32[256]{0:T(256)S(1)} %compare_convert_fusion.1), channel_id=1, source_target_pairs={{0,256},{64,320},{128,384},{192,448},{256,0},{320,64},{384,128},{4... | collective-permute-start | bytes 3080 | tf_op jit(solution)/shard_map/ppermute | solution.py:12
  160.4 219.6 %copy-start.1 = (bf16[256,256]{1,0:T(8,128)(2,1)S(1)}, bf16[256,256]{1,0:T(8,128)(2,1)}, u32[]{:S(2)}) copy-start(bf16[256,256]{1,0:T(8,128)(2,1)} %param.14) | copy-start | bytes 393220
  162.3 370.2 %all-reduce.7.cloned.1.call-start = ((), (), s32[]{:S(2)}) async-start(), calls=%async_computation.3 | async-start | bytes 786432 | tf_op jit(solution)/shard_map/psum | solution.py:63
  312.3 69.6 %copy-start = (f32[256,256]{1,0:T(8,128)S(1)}, f32[256,256]{1,0:T(8,128)}, u32[]{:S(2)}) copy-start(f32[256,256]{1,0:T(8,128)} %all-reduce.5.cloned.1.call-done) | copy-start | bytes 786436
  381.9 162.7 %collective-permute-start.3 = (f32[256,256]{1,0:T(8,128)S(1)}, f32[256,256]{1,0:T(8,128)S(1)}, u32[]{:S(2)}, u32[]{:S(2)}) collective-permute-start(f32[256,256]{1,0:T(8,128)S(1)} %copy-done), channel_id=1, source_target_pairs={{0,64},{64,0},{128,192},{192,128},{256,320},{320,256},{384,448},{4... | collective-permute-start | bytes 786440 | tf_op jit(solution)/shard_map/ppermute | solution.py:12
  532.5 3.4 collective-permute-start.1
  535.9 19.1 %collective-permute-start.2 = (f32[256,256]{1,0:T(8,128)}, f32[256,256]{1,0:T(8,128)S(1)}, u32[]{:S(2)}, u32[]{:S(2)}) collective-permute-start(f32[256,256]{1,0:T(8,128)} %get-tuple-element.103), channel_id=1, source_target_pairs={{0,64},{64,0},{128,192},{192,128},{256,320},{320,256},{384,448},{4... | collective-permute-start | bytes 786440 | tf_op jit(solution)/shard_map/ppermute | solution.py:12
  541.2 7.7 collective-permute-start.5
  549.6 72.3 %copy-start.3 = (f32[256,256]{1,0:T(8,128)S(1)}, f32[256,256]{1,0:T(8,128)}, u32[]{:S(2)}) copy-start(f32[256,256]{1,0:T(8,128)} %get-tuple-element.103) | copy-start | bytes 786436
  549.8 75.2 %collective-permute-start.9 = (bf16[256,64]{1,0:T(8,128)(2,1)S(1)}, bf16[256,64]{1,0:T(8,128)(2,1)S(1)}, u32[]{:S(2)}, u32[]{:S(2)}) collective-permute-start(bf16[256,64]{1,0:T(8,128)(2,1)S(1)} %get-tuple-element.106), channel_id=1, source_target_pairs={{0,256},{64,320},{128,384},{192,448},{256,0},{320,64},{384,128},{4... | collective-permute-start | bytes 98312 | tf_op jit(solution)/shard_map/ppermute | solution.py:12
  599.8 41.5 %copy-start.10 = (s32[2,2]{1,0:T(2,128)}, s32[2,2]{1,0:T(2,128)S(1)}, u32[]{:S(2)}) copy-start(s32[2,2]{1,0:T(2,128)S(1)} %get-tuple-element.382) | copy-start | bytes 52
  622.5 11.1 %collective-permute-start.6 = (f32[256,256]{1,0:T(8,128)S(1)}, f32[256,256]{1,0:T(8,128)S(1)}, u32[]{:S(2)}, u32[]{:S(2)}) collective-permute-start(f32[256,256]{1,0:T(8,128)S(1)} %fusion.19), channel_id=1, source_target_pairs={{0,128},{64,192},{128,0},{192,64},{256,384},{320,448},{384,256},{4... | collective-permute-start | bytes 786440 | tf_op jit(solution)/shard_map/ppermute | solution.py:12
  625.1 12.4 %collective-permute-start.7 = (f32[256,256]{1,0:T(8,128)S(1)}, f32[256,256]{1,0:T(8,128)S(1)}, u32[]{:S(2)}, u32[]{:S(2)}) collective-permute-start(f32[256,256]{1,0:T(8,128)S(1)} %get-tuple-element.112), channel_id=1, source_target_pairs={{0,128},{64,192},{128,0},{192,64},{256,384},{320,448},{384,256},{4... | collective-permute-start | bytes 786440 | tf_op jit(solution)/shard_map/ppermute | solution.py:12
  633.7 5.5 copy-start.7
  663.7 61.6 %copy-start.8 = (pred[256]{0:T(512)(128)(4,1)S(1)}, pred[256]{0:T(512)(128)(4,1)}, u32[]{:S(2)}) copy-start(pred[256]{0:T(512)(128)(4,1)} %get-tuple-element.154) | copy-start | bytes 772
  706.0 58.8 %copy-start.11 = (s32[2,2]{1,0:T(2,128)S(1)}, s32[2,2]{1,0:T(2,128)}, u32[]{:S(2)}) copy-start(s32[2,2]{1,0:T(2,128)} %get-tuple-element.383) | copy-start | bytes 52
  708.1 60.7 %copy-start.4 = (f32[256,256]{1,0:T(8,128)}, f32[256,256]{1,0:T(8,128)S(1)}, u32[]{:S(2)}) copy-start(f32[256,256]{1,0:T(8,128)S(1)} %fusion.25) | copy-start | bytes 786436
  708.1 12.6 %collective-permute-start.10 = (f32[256,256]{1,0:T(8,128)S(1)}, f32[256,256]{1,0:T(8,128)S(1)}, u32[]{:S(2)}, u32[]{:S(2)}) collective-permute-start(f32[256,256]{1,0:T(8,128)S(1)} %fusion.25), channel_id=1, source_target_pairs={{0,256},{64,320},{128,384},{192,448},{256,0},{320,64},{384,128},{4... | collective-permute-start | bytes 786440 | tf_op jit(solution)/shard_map/ppermute | solution.py:12
  710.9 12.7 %collective-permute-start.11 = (f32[256,256]{1,0:T(8,128)S(1)}, f32[256,256]{1,0:T(8,128)S(1)}, u32[]{:S(2)}, u32[]{:S(2)}) collective-permute-start(f32[256,256]{1,0:T(8,128)S(1)} %get-tuple-element.108), channel_id=1, source_target_pairs={{0,256},{64,320},{128,384},{192,448},{256,0},{320,64},{384,128},{4... | collective-permute-start | bytes 786440 | tf_op jit(solution)/shard_map/ppermute | solution.py:12
  720.7 2.9 copy-start.6
  768.8 23.9 %copy-start.5 = (f32[256,256]{1,0:T(8,128)S(1)}, f32[256,256]{1,0:T(8,128)}, u32[]{:S(2)}) copy-start(f32[256,256]{1,0:T(8,128)} %copy-done.4) | copy-start | bytes 786436
Sparse Core Ops, SparseCore 0:
  11.1 140.5 all-gather.1
  162.4 149.8 all-reduce.4
  381.2 151.2 all-reduce.6
